TPU v7x, 128 devices: a whole 4x4x4 slice. The times are simulated.
128 devices in a mesh: day: 32 (over z, x, core), pt: 4 (over y).
Axes of the slice: x: 4, y: 4, z: 4, core: 2. Of those that a mesh axis runs over, the one named last changes fastest.
Arguments:
- points: bfloat16 [32, 64, 2048], P('day', None, 'pt'), may hold values from -0.45 to 0.45
- cells: bfloat16 [32, 64, 8192], P('day', None, 'pt'), may hold values from -0.44921875 to 0.44921875
- clone_weight: float32 [32, 64, 2048], P('day', None, 'pt'), may hold values from 0.1 to 1
- potential: float32 [32, 2048], P('day', 'pt'), may hold values from 0.2 to 5
- support_count: int32 [32], P('day'), may hold values from 512 to 2048, as said below
- cell_count: int32 [32], P('day'), may hold values from 2048 to 8192, as said below
Outputs:
- forward_message: float32 [32, 64, 2048], P('day', None, 'pt')
- backward_message: float32 [32, 64, 2048], P('day', None, 'pt')
- fit_ratio: float32 [32, 2048], P('day', 'pt')
Inputs may be any that keep to these rules, and one draw needn't show every extreme that they name: Live support points of a day are its first support_count slots; some day has all 2048 slots live and some day has 512. Observed cells of a day are its first cell_count slots; some day fills all 8192 slots and some day has 2048.
All inputs are finite; a program needn't handle non-finite values.
Results may differ from a plain program's by a relative error of at most 0.0003.
Values may be sent and summed in bfloat16 or wider, within the bound.
A program may use at most 64 MiB of HBM per device.

v0:
```python
import jax
import jax.numpy as jnp
from jax import lax
from jax.sharding import PartitionSpec as P


def with_halo(cells, sides, width):
    for axis, dim in sides:
        count = lax.axis_size(axis)
        ends = count - 1
        head = lax.slice_in_dim(cells, 0, width, axis=dim)
        tail = lax.slice_in_dim(cells, cells.shape[dim] - width, cells.shape[dim], axis=dim)
        cells = jnp.concatenate(
            [
                lax.ppermute(tail, axis, [(i, (i + 1) % count) for i in range(ends)]),
                cells,
                lax.ppermute(head, axis, [((i + 1) % count, i) for i in range(ends)]),
            ],
            axis=dim,
        )
    return cells


def shifted(block, axis, distance):
    devices = range(lax.axis_size(axis))
    route = [(i - distance, i) for i in devices if i - distance in devices]
    return lax.ppermute(block, axis, route)


def norm_of(coords):
    wide = coords.astype(jnp.float32)
    return jnp.sum(wide * wide, axis=0)


def squared_dist(left_pts, left_norm, right_pts, right_norm):
    inner = lax.dot_general(
        left_pts, right_pts, (((0,), (0,)), ((), ())), preferred_element_type=jnp.float32
    )
    return left_norm[:, None] + right_norm[None, :] - 2.0 * inner


def shards(points, cells, clone_weight, potential, support_count, cell_count):
    pt_rank = lax.axis_index("pt")
    day_index = lax.axis_index("day")
    day_count = lax.axis_size("day")
    full_pts, full_clone, full_pot = (
        lax.all_gather(points.astype(jnp.float32), "pt", axis=2, tiled=True).astype(points.dtype),
        lax.all_gather(clone_weight, "pt", axis=2, tiled=True),
        lax.all_gather(potential, "pt", axis=1, tiled=True),
    )
    beside_all = with_halo(full_pts, (("day", 0),), 1)
    before_day = beside_all[0]
    after_day = beside_all[2]
    own_pts = points[0]
    per_device = own_pts.shape[1]
    support_total = full_pts.shape[2]
    clones = clone_weight.shape[1]
    weight = full_clone[0] * full_pot
    live_total = support_count[0].astype(jnp.float32)
    live_all = (jnp.arange(support_total, dtype=jnp.int32) < support_count[0]).astype(jnp.float32)
    live_own = lax.dynamic_slice_in_dim(live_all, pt_rank * per_device, per_device)
    own_norm = norm_of(own_pts)
    before_norm = norm_of(before_day)
    after_norm = norm_of(after_day)
    row_span = 512
    span_count = support_total // row_span

    def kernel_rows(source_pts, source_norm, block_index):
        offset = block_index * row_span
        source_rows = lax.dynamic_slice_in_dim(source_pts, offset, row_span, 1)
        norm_rows = lax.dynamic_slice_in_dim(source_norm, offset, row_span, 0)
        return jnp.exp(-squared_dist(source_rows, norm_rows, own_pts, own_norm)).astype(
            jnp.bfloat16
        )

    def contract(sent_rows, source_pts, source_norm):

        def add_rows(block_index, result):
            sent_part = lax.dynamic_slice_in_dim(sent_rows, block_index * row_span, row_span, 1)
            return result + jnp.dot(
                sent_part,
                kernel_rows(source_pts, source_norm, block_index),
                preferred_element_type=jnp.float32,
            )

        return lax.fori_loop(
            0, span_count, add_rows, jnp.zeros((sent_rows.shape[0], per_device), jnp.float32)
        )

    block_count = 4
    block_rows = clones // block_count
    steps_total = day_count + block_count - 1
    empty_rows = jnp.zeros((block_rows, per_device), jnp.float32)
    seed_rows = jnp.broadcast_to(live_own[None, :], (block_rows, per_device))

    def settle(piece_rows, full_rows, valid):
        column_sums = jnp.sum(full_rows * live_all[None, :], axis=1, keepdims=True)
        column_sums = jnp.where(valid, column_sums, 1.0)
        own_part = piece_rows * live_own[None, :] * live_total / column_sums
        whole_part = full_rows * live_all[None, :] * live_total / column_sums
        return (own_part, whole_part)

    def one_step(step_index, carried):
        forward_in, backward_in, forward_out, backward_out = carried
        forward_at = step_index - day_index
        forward_ok = (forward_at >= 0) & (forward_at < block_count)
        forward_block = jnp.clip(forward_at, 0, block_count - 1)
        backward_at = step_index - (day_count - 1 - day_index)
        backward_ok = (backward_at >= 0) & (backward_at < block_count)
        backward_block = jnp.clip(backward_at, 0, block_count - 1)
        forward_got = lax.cond(
            forward_ok & (day_index > 0),
            lambda: contract(forward_in, before_day, before_norm),
            lambda: empty_rows,
        )
        forward_piece = jnp.where(day_index == 0, seed_rows, forward_got)
        backward_got = lax.cond(
            backward_ok & (day_index < day_count - 1),
            lambda: contract(backward_in, after_day, after_norm),
            lambda: empty_rows,
        )
        backward_piece = jnp.where(day_index == day_count - 1, seed_rows, backward_got)
        forward_full, backward_full = (
            lax.all_gather(forward_piece, "pt", axis=1, tiled=True),
            lax.all_gather(backward_piece, "pt", axis=1, tiled=True),
        )
        forward_own, forward_all = settle(forward_piece, forward_full, forward_ok)
        backward_own, backward_all = settle(backward_piece, backward_full, backward_ok)
        forward_out = jnp.where(
            forward_ok,
            lax.dynamic_update_slice_in_dim(
                forward_out, forward_own, forward_block * block_rows, 0
            ),
            forward_out,
        )
        backward_out = jnp.where(
            backward_ok,
            lax.dynamic_update_slice_in_dim(
                backward_out, backward_own, backward_block * block_rows, 0
            ),
            backward_out,
        )
        forward_sent = (
            forward_all
            * lax.dynamic_slice_in_dim(weight, forward_block * block_rows, block_rows, 0)
        ).astype(jnp.bfloat16)
        backward_sent = (
            backward_all
            * lax.dynamic_slice_in_dim(weight, backward_block * block_rows, block_rows, 0)
        ).astype(jnp.bfloat16)
        forward_in = shifted(forward_sent, "day", 1)
        backward_in = shifted(backward_sent, "day", -1)
        return (forward_in, backward_in, forward_out, backward_out)

    start_in = jnp.zeros((block_rows, support_total), jnp.bfloat16)
    start_out = jnp.zeros((clones, per_device), jnp.float32)
    carried = lax.fori_loop(0, steps_total, one_step, (start_in, start_in, start_out, start_out))
    forward_out = carried[2]
    backward_out = carried[3]
    mass_own = (
        live_own * potential[0] * jnp.sum(forward_out * clone_weight[0] * backward_out, axis=0)
    )
    cell_total = cell_count[0]
    cell_total_f = cell_total.astype(jnp.float32)
    all_cells = lax.all_gather(cells, "pt", axis=2, tiled=True)[0]
    cell_slots = all_cells.shape[1]
    cell_norm = norm_of(all_cells)
    fit_span = 512
    fit_blocks = cell_slots // fit_span

    def fit_columns(block_index):
        offset = block_index * fit_span
        chosen = lax.dynamic_slice_in_dim(all_cells, offset, fit_span, 1)
        chosen_norm = lax.dynamic_slice_in_dim(cell_norm, offset, fit_span, 0)
        return jnp.exp(-squared_dist(own_pts, own_norm, chosen, chosen_norm))

    def density_part(block_index):
        return jnp.dot(mass_own, fit_columns(block_index), precision=lax.Precision.HIGHEST)

    partial_density = lax.map(density_part, jnp.arange(fit_blocks)).reshape(cell_slots)
    column_sums, mass_total = lax.psum((partial_density, jnp.sum(mass_own)), "pt")
    density = column_sums / mass_total
    cell_live = (jnp.arange(cell_slots, dtype=jnp.int32) < cell_total).astype(jnp.float32)
    inverse = cell_live / density

    def ratio_part(block_index, running):
        chosen_inverse = lax.dynamic_slice_in_dim(inverse, block_index * fit_span, fit_span, 0)
        return running + jnp.dot(
            fit_columns(block_index), chosen_inverse, precision=lax.Precision.HIGHEST
        )

    summed = lax.fori_loop(0, fit_blocks, ratio_part, jnp.zeros((per_device,), jnp.float32))
    fit_rows_out = live_own / cell_total_f * summed
    return (forward_out[None], backward_out[None], fit_rows_out[None])


def solution(mesh):
    in_specs = (
        P("day", None, "pt"),
        P("day", None, "pt"),
        P("day", None, "pt"),
        P("day", "pt"),
        P("day"),
        P("day"),
    )
    out_specs = (P("day", None, "pt"), P("day", None, "pt"), P("day", "pt"))
    return jax.shard_map(shards, mesh=mesh, in_specs=in_specs, out_specs=out_specs, check_vma=False)
```

profile of v0, /device:TPU:1, one launch (start us, length us, event | category | flops | bytes accessed | tf_op | source)
XLA Modules:
  0.0 1604.9 jit_solution(1951104666775304493)
XLA Ops:
  7.2 11.5 all_gather.28
  26.8 11.7 all_gather.29
  49.3 1439.7 %while.76 = (s32[]{:T(128)}, bf16[16,2048]{1,0:T(8,128)(2,1)S(1)}, bf16[16,2048]{1,0:T(8,128)(2,1)S(1)}, f32[64,512]{1,0:T(8,128)S(1)}, f32[64,512]{1,0:T(8,128)...) while((s32[]{:T(128)}, bf16[16,2048]{1,0:T(8,128)(2,1)S(1)}, ...), condition=%wide.region_14.15_spmd.clone.clone, body=%wide.region_3.14_spmd.clone.clone.sunk | while | flops 87085088 | bytes 2573997 | solution.py:157
  70.5 11.3 collective-permute-start
  140.0 9.2 all_gather.39
  246.9 9.2 all_gather.38
  256.1 9.5 all_gather.39
  266.6 13.6 collective-permute-start
  287.7 9.2 all_gather.38
  296.9 9.5 all_gather.39
  331.3 9.5 all_gather.39
  356.5 9.2 all_gather.38
  365.7 9.5 all_gather.39
  376.1 9.3 collective-permute-start
  402.2 9.4 all_gather.39
  427.4 9.2 all_gather.38
  436.6 9.5 all_gather.39
  470.9 9.4 all_gather.39
  481.3 11.4 collective-permute-start
  500.3 9.2 all_gather.38
  509.4 9.4 all_gather.39
  534.7 9.2 all_gather.38
  553.8 12.3 collective-permute-start
  573.8 9.2 all_gather.38
  593.0 16.1 %collective-permute-start = (bf16[16,2048]{1,0:T(8,128)(2,1)S(1)}, bf16[16,2048]{1,0:T(8,128)(2,1)S(1)}, u32[]{:S(2)}, u32[]{:S(2)}) collective-permute-start(bf16[16,2048]{1,0:T(8,128)(2,1)S(1)} %get-tuple-element.1416), channel_id=1, source_target_pairs={{0,4},{4,8},{8,12},{12,16},{16,20},{20,24},{24,28},{28,32},{32,36}... | collective-permute-start | bytes 196616 | tf_op jit(solution)/shard_map/while/body/eval_jaxpr/ppermute | solution.py:27
  635.9 9.7 collective-permute-start
  672.4 9.7 collective-permute-start
  708.8 9.7 collective-permute-start
  745.3 9.7 collective-permute-start
  781.8 9.7 collective-permute-start
  799.1 9.2 all_gather.38
  818.3 21.3 %collective-permute-start = (bf16[16,2048]{1,0:T(8,128)(2,1)S(1)}, bf16[16,2048]{1,0:T(8,128)(2,1)S(1)}, u32[]{:S(2)}, u32[]{:S(2)}) collective-permute-start(bf16[16,2048]{1,0:T(8,128)(2,1)S(1)} %get-tuple-element.1416), channel_id=1, source_target_pairs={{0,4},{4,8},{8,12},{12,16},{16,20},{20,24},{24,28},{28,32},{32,36}... | collective-permute-start | bytes 196616 | tf_op jit(solution)/shard_map/while/body/eval_jaxpr/ppermute | solution.py:27
  847.2 9.2 all_gather.38
  866.4 16.0 collective-permute-start
  909.3 20.5 %collective-permute-start = (bf16[16,2048]{1,0:T(8,128)(2,1)S(1)}, bf16[16,2048]{1,0:T(8,128)(2,1)S(1)}, u32[]{:S(2)}, u32[]{:S(2)}) collective-permute-start(bf16[16,2048]{1,0:T(8,128)(2,1)S(1)} %get-tuple-element.1416), channel_id=1, source_target_pairs={{0,4},{4,8},{8,12},{12,16},{16,20},{20,24},{24,28},{28,32},{32,36}... | collective-permute-start | bytes 196616 | tf_op jit(solution)/shard_map/while/body/eval_jaxpr/ppermute | solution.py:27
  956.6 29.0 %collective-permute-start = (bf16[16,2048]{1,0:T(8,128)(2,1)S(1)}, bf16[16,2048]{1,0:T(8,128)(2,1)S(1)}, u32[]{:S(2)}, u32[]{:S(2)}) collective-permute-start(bf16[16,2048]{1,0:T(8,128)(2,1)S(1)} %get-tuple-element.1416), channel_id=1, source_target_pairs={{0,4},{4,8},{8,12},{12,16},{16,20},{20,24},{24,28},{28,32},{32,36}... | collective-permute-start | bytes 196616 | tf_op jit(solution)/shard_map/while/body/eval_jaxpr/ppermute | solution.py:27
  1012.4 22.4 %collective-permute-start = (bf16[16,2048]{1,0:T(8,128)(2,1)S(1)}, bf16[16,2048]{1,0:T(8,128)(2,1)S(1)}, u32[]{:S(2)}, u32[]{:S(2)}) collective-permute-start(bf16[16,2048]{1,0:T(8,128)(2,1)S(1)} %get-tuple-element.1416), channel_id=1, source_target_pairs={{0,4},{4,8},{8,12},{12,16},{16,20},{20,24},{24,28},{28,32},{32,36}... | collective-permute-start | bytes 196616 | tf_op jit(solution)/shard_map/while/body/eval_jaxpr/ppermute | solution.py:27
  1061.6 28.9 %collective-permute-start = (bf16[16,2048]{1,0:T(8,128)(2,1)S(1)}, bf16[16,2048]{1,0:T(8,128)(2,1)S(1)}, u32[]{:S(2)}, u32[]{:S(2)}) collective-permute-start(bf16[16,2048]{1,0:T(8,128)(2,1)S(1)} %get-tuple-element.1416), channel_id=1, source_target_pairs={{0,4},{4,8},{8,12},{12,16},{16,20},{20,24},{24,28},{28,32},{32,36}... | collective-permute-start | bytes 196616 | tf_op jit(solution)/shard_map/while/body/eval_jaxpr/ppermute | solution.py:27
  1117.3 22.7 %collective-permute-start = (bf16[16,2048]{1,0:T(8,128)(2,1)S(1)}, bf16[16,2048]{1,0:T(8,128)(2,1)S(1)}, u32[]{:S(2)}, u32[]{:S(2)}) collective-permute-start(bf16[16,2048]{1,0:T(8,128)(2,1)S(1)} %get-tuple-element.1416), channel_id=1, source_target_pairs={{0,4},{4,8},{8,12},{12,16},{16,20},{20,24},{24,28},{28,32},{32,36}... | collective-permute-start | bytes 196616 | tf_op jit(solution)/shard_map/while/body/eval_jaxpr/ppermute | solution.py:27
  1156.8 9.4 all_gather.39
  1167.2 22.2 %collective-permute-start = (bf16[16,2048]{1,0:T(8,128)(2,1)S(1)}, bf16[16,2048]{1,0:T(8,128)(2,1)S(1)}, u32[]{:S(2)}, u32[]{:S(2)}) collective-permute-start(bf16[16,2048]{1,0:T(8,128)(2,1)S(1)} %get-tuple-element.1416), channel_id=1, source_target_pairs={{0,4},{4,8},{8,12},{12,16},{16,20},{20,24},{24,28},{28,32},{32,36}... | collective-permute-start | bytes 196616 | tf_op jit(solution)/shard_map/while/body/eval_jaxpr/ppermute | solution.py:27
  1216.2 22.6 %collective-permute-start = (bf16[16,2048]{1,0:T(8,128)(2,1)S(1)}, bf16[16,2048]{1,0:T(8,128)(2,1)S(1)}, u32[]{:S(2)}, u32[]{:S(2)}) collective-permute-start(bf16[16,2048]{1,0:T(8,128)(2,1)S(1)} %get-tuple-element.1416), channel_id=1, source_target_pairs={{0,4},{4,8},{8,12},{12,16},{16,20},{20,24},{24,28},{28,32},{32,36}... | collective-permute-start | bytes 196616 | tf_op jit(solution)/shard_map/while/body/eval_jaxpr/ppermute | solution.py:27
  1248.2 9.4 all_gather.38
  1267.7 20.4 %collective-permute-start = (bf16[16,2048]{1,0:T(8,128)(2,1)S(1)}, bf16[16,2048]{1,0:T(8,128)(2,1)S(1)}, u32[]{:S(2)}, u32[]{:S(2)}) collective-permute-start(bf16[16,2048]{1,0:T(8,128)(2,1)S(1)} %get-tuple-element.1416), channel_id=1, source_target_pairs={{0,4},{4,8},{8,12},{12,16},{16,20},{20,24},{24,28},{28,32},{32,36}... | collective-permute-start | bytes 196616 | tf_op jit(solution)/shard_map/while/body/eval_jaxpr/ppermute | solution.py:27
  1433.8 9.4 all_gather.39
  1491.2 52.7 %while.74 = (s32[]{:T(128)}, f32[16,512]{1,0:T(8,128)S(1)}, f32[512]{0:T(512)S(1)}, s32[16]{0:T(128)S(1)}, f32[8192]{0:T(1024)S(1)}, /*index=5*/bf16[64,8192]{1,...) while((s32[]{:T(128)}, f32[16,512]{1,0:T(8,128)S(1)}, ...), condition=%wide.region_20.21_spmd, body=%wide.region_19.20_spmd.sunk | while | flops 37748740 | bytes 2244795 | solution.py:180
  1544.0 14.2 all-reduce
  1558.9 38.6 %while.75 = (s32[]{:T(128)}, f32[512]{0:T(512)S(1)}, f32[512]{0:T(512)S(1)}, f32[8192]{0:T(1024)S(1)}, bf16[64,8192]{1,0:T(8,128)(2,1)}, /*index=5*/bf16[64,512]...) while((s32[]{:T(128)}, f32[512]{0:T(512)S(1)}, ...), condition=%wide.region_23.24_spmd.clone, body=%wide.region_22.23_spmd.clone.sunk | while | flops 37749764 | bytes 2250929 | solution.py:192
  (786 shorter events, 1145.5 us)
Async XLA Ops:
  7.2 1482.5 %all-gather.2.cloned.1.call-start = ((), (), s32[]{:S(2)}) async-start(), calls=%async_computation | async-start | bytes 1310720 | tf_op jit(solution)/shard_map/all_gather | solution.py:165
  18.7 30.4 %collective-permute-start.3 = (bf16[1,64,2048]{2,1,0:T(8,128)(2,1)S(1)}, bf16[1,64,2048]{2,1,0:T(8,128)(2,1)S(1)}, u32[]{:S(2)}, u32[]{:S(2)}) collective-permute-start(bf16[1,64,2048]{2,1,0:T(8,128)(2,1)S(1)} %all_gather.28), channel_id=1, source_target_pairs={{4,0},{8,4},{12,8},{16,12},{20,16},{24,20},{28,24},{32,28},{36,32}... | collective-permute-start | bytes 786440 | tf_op jit(solution)/shard_map/ppermute | solution.py:17
  23.8 25.4 %collective-permute-start.2 = (bf16[1,64,2048]{2,1,0:T(8,128)(2,1)S(1)}, bf16[1,64,2048]{2,1,0:T(8,128)(2,1)S(1)}, u32[]{:S(2)}, u32[]{:S(2)}) collective-permute-start(bf16[1,64,2048]{2,1,0:T(8,128)(2,1)S(1)} %all_gather.28), channel_id=1, source_target_pairs={{0,4},{4,8},{8,12},{12,16},{16,20},{20,24},{24,28},{28,32},{32,36}... | collective-permute-start | bytes 786440 | tf_op jit(solution)/shard_map/ppermute | solution.py:15
  70.5 13.3 collective-permute-start
  81.8 5.6 collective-permute-start.1
  116.9 5.6 collective-permute-start.1
  150.2 9.6 collective-permute-start
  157.7 5.6 collective-permute-start.1
  190.9 9.7 collective-permute-start
  198.5 5.6 collective-permute-start.1
  231.7 9.7 collective-permute-start
  266.6 15.6 collective-permute-start
  307.4 9.2 collective-permute-start
  314.5 5.6 collective-permute-start.1
  341.7 9.2 collective-permute-start
  348.9 5.6 collective-permute-start.1
  376.1 11.4 collective-permute-start
  385.4 5.6 collective-permute-start.1
  412.5 9.3 collective-permute-start
  419.8 5.6 collective-permute-start.1
  447.0 9.2 collective-permute-start
  454.2 5.6 collective-permute-start.1
  481.3 13.4 collective-permute-start
  519.8 9.3 collective-permute-start
  553.8 14.3 collective-permute-start
  593.0 18.1 %collective-permute-start = (bf16[16,2048]{1,0:T(8,128)(2,1)S(1)}, bf16[16,2048]{1,0:T(8,128)(2,1)S(1)}, u32[]{:S(2)}, u32[]{:S(2)}) collective-permute-start(bf16[16,2048]{1,0:T(8,128)(2,1)S(1)} %get-tuple-element.1416), channel_id=1, source_target_pairs={{0,4},{4,8},{8,12},{12,16},{16,20},{20,24},{24,28},{28,32},{32,36}... | collective-permute-start | bytes 196616 | tf_op jit(solution)/shard_map/while/body/eval_jaxpr/ppermute | solution.py:27
  635.9 11.7 collective-permute-start
  672.4 11.7 collective-permute-start
  708.8 11.7 collective-permute-start
  745.3 11.7 collective-permute-start
  781.8 11.7 collective-permute-start
  818.3 23.4 %collective-permute-start = (bf16[16,2048]{1,0:T(8,128)(2,1)S(1)}, bf16[16,2048]{1,0:T(8,128)(2,1)S(1)}, u32[]{:S(2)}, u32[]{:S(2)}) collective-permute-start(bf16[16,2048]{1,0:T(8,128)(2,1)S(1)} %get-tuple-element.1416), channel_id=1, source_target_pairs={{0,4},{4,8},{8,12},{12,16},{16,20},{20,24},{24,28},{28,32},{32,36}... | collective-permute-start | bytes 196616 | tf_op jit(solution)/shard_map/while/body/eval_jaxpr/ppermute | solution.py:27
  866.4 18.0 %collective-permute-start = (bf16[16,2048]{1,0:T(8,128)(2,1)S(1)}, bf16[16,2048]{1,0:T(8,128)(2,1)S(1)}, u32[]{:S(2)}, u32[]{:S(2)}) collective-permute-start(bf16[16,2048]{1,0:T(8,128)(2,1)S(1)} %get-tuple-element.1416), channel_id=1, source_target_pairs={{0,4},{4,8},{8,12},{12,16},{16,20},{20,24},{24,28},{28,32},{32,36}... | collective-permute-start | bytes 196616 | tf_op jit(solution)/shard_map/while/body/eval_jaxpr/ppermute | solution.py:27
  909.3 22.6 %collective-permute-start = (bf16[16,2048]{1,0:T(8,128)(2,1)S(1)}, bf16[16,2048]{1,0:T(8,128)(2,1)S(1)}, u32[]{:S(2)}, u32[]{:S(2)}) collective-permute-start(bf16[16,2048]{1,0:T(8,128)(2,1)S(1)} %get-tuple-element.1416), channel_id=1, source_target_pairs={{0,4},{4,8},{8,12},{12,16},{16,20},{20,24},{24,28},{28,32},{32,36}... | collective-permute-start | bytes 196616 | tf_op jit(solution)/shard_map/while/body/eval_jaxpr/ppermute | solution.py:27
  956.6 31.0 %collective-permute-start = (bf16[16,2048]{1,0:T(8,128)(2,1)S(1)}, bf16[16,2048]{1,0:T(8,128)(2,1)S(1)}, u32[]{:S(2)}, u32[]{:S(2)}) collective-permute-start(bf16[16,2048]{1,0:T(8,128)(2,1)S(1)} %get-tuple-element.1416), channel_id=1, source_target_pairs={{0,4},{4,8},{8,12},{12,16},{16,20},{20,24},{24,28},{28,32},{32,36}... | collective-permute-start | bytes 196616 | tf_op jit(solution)/shard_map/while/body/eval_jaxpr/ppermute | solution.py:27
  1012.4 24.5 %collective-permute-start = (bf16[16,2048]{1,0:T(8,128)(2,1)S(1)}, bf16[16,2048]{1,0:T(8,128)(2,1)S(1)}, u32[]{:S(2)}, u32[]{:S(2)}) collective-permute-start(bf16[16,2048]{1,0:T(8,128)(2,1)S(1)} %get-tuple-element.1416), channel_id=1, source_target_pairs={{0,4},{4,8},{8,12},{12,16},{16,20},{20,24},{24,28},{28,32},{32,36}... | collective-permute-start | bytes 196616 | tf_op jit(solution)/shard_map/while/body/eval_jaxpr/ppermute | solution.py:27
  1061.6 30.9 %collective-permute-start = (bf16[16,2048]{1,0:T(8,128)(2,1)S(1)}, bf16[16,2048]{1,0:T(8,128)(2,1)S(1)}, u32[]{:S(2)}, u32[]{:S(2)}) collective-permute-start(bf16[16,2048]{1,0:T(8,128)(2,1)S(1)} %get-tuple-element.1416), channel_id=1, source_target_pairs={{0,4},{4,8},{8,12},{12,16},{16,20},{20,24},{24,28},{28,32},{32,36}... | collective-permute-start | bytes 196616 | tf_op jit(solution)/shard_map/while/body/eval_jaxpr/ppermute | solution.py:27
  1117.3 24.7 %collective-permute-start = (bf16[16,2048]{1,0:T(8,128)(2,1)S(1)}, bf16[16,2048]{1,0:T(8,128)(2,1)S(1)}, u32[]{:S(2)}, u32[]{:S(2)}) collective-permute-start(bf16[16,2048]{1,0:T(8,128)(2,1)S(1)} %get-tuple-element.1416), channel_id=1, source_target_pairs={{0,4},{4,8},{8,12},{12,16},{16,20},{20,24},{24,28},{28,32},{32,36}... | collective-permute-start | bytes 196616 | tf_op jit(solution)/shard_map/while/body/eval_jaxpr/ppermute | solution.py:27
  1167.2 24.3 %collective-permute-start = (bf16[16,2048]{1,0:T(8,128)(2,1)S(1)}, bf16[16,2048]{1,0:T(8,128)(2,1)S(1)}, u32[]{:S(2)}, u32[]{:S(2)}) collective-permute-start(bf16[16,2048]{1,0:T(8,128)(2,1)S(1)} %get-tuple-element.1416), channel_id=1, source_target_pairs={{0,4},{4,8},{8,12},{12,16},{16,20},{20,24},{24,28},{28,32},{32,36}... | collective-permute-start | bytes 196616 | tf_op jit(solution)/shard_map/while/body/eval_jaxpr/ppermute | solution.py:27
  1216.2 24.6 %collective-permute-start = (bf16[16,2048]{1,0:T(8,128)(2,1)S(1)}, bf16[16,2048]{1,0:T(8,128)(2,1)S(1)}, u32[]{:S(2)}, u32[]{:S(2)}) collective-permute-start(bf16[16,2048]{1,0:T(8,128)(2,1)S(1)} %get-tuple-element.1416), channel_id=1, source_target_pairs={{0,4},{4,8},{8,12},{12,16},{16,20},{20,24},{24,28},{28,32},{32,36}... | collective-permute-start | bytes 196616 | tf_op jit(solution)/shard_map/while/body/eval_jaxpr/ppermute | solution.py:27
  1238.8 7.4 collective-permute-start.1
  1267.7 22.4 %collective-permute-start = (bf16[16,2048]{1,0:T(8,128)(2,1)S(1)}, bf16[16,2048]{1,0:T(8,128)(2,1)S(1)}, u32[]{:S(2)}, u32[]{:S(2)}) collective-permute-start(bf16[16,2048]{1,0:T(8,128)(2,1)S(1)} %get-tuple-element.1416), channel_id=1, source_target_pairs={{0,4},{4,8},{8,12},{12,16},{16,20},{20,24},{24,28},{28,32},{32,36}... | collective-permute-start | bytes 196616 | tf_op jit(solution)/shard_map/while/body/eval_jaxpr/ppermute | solution.py:27
  1321.3 9.8 collective-permute-start
  1362.3 9.6 collective-permute-start
  1403.1 9.6 collective-permute-start
  1444.2 6.3 collective-permute-start
  1472.8 15.4 collective-permute-start
  1480.5 8.5 collective-permute-start.1
  (30 other events, 1644.2 us)
Sparse Core Ops, SparseCore 0:
  26.9 23.9 all-gather.1
where the time goes:
time: 1620 us; the launch traced here: 1600 us
  blocking collectives  689 us (43%)
  starting transfers between devices  526 us (32%)
  waiting for transfers between devices  121 us (7%)
  matrix products  119 us (7%)
  other arithmetic  65.8 us (4%)
  local copies, waits for them, and re-layouts  55.5 us (3%)
    ppermute x70, starting transfers between devices, shifted(): return lax.ppermute(block, axis, route)  517 us
    all_gather x35, blocking collectives, one_step(): lax.all_gather(forward_piece, 'pt', axis=1, tiled=True)  322 us
    all_gather x35, blocking collectives, one_step(): lax.all_gather(backward_piece, 'pt', axis=1, tiled=True)  320 us
    ppermute x70, waiting for transfers between devices, shifted(): return lax.ppermute(block, axis, route)  121 us
    dot_general x32, matrix products, add_rows(): jnp.dot(sent_part, kernel_rows(source_pts, source_norm, block_index), pre...  53.9 us
    dot_general x32, matrix products, squared_dist(): lax.dot_general(left_pts, right_pts, (((0,), (0,)), ((), ())), preferred_...  39 us
    another operation x62, local copies, waits for them, and re-layouts  38.3 us
  transfers between devices with their start and end apart: 73, of which 35 were waited for; matrix products, arithmetic and copies ran while one was open for 10% of the time, Pallas kernels for 0%

commit v1 on v0

v1 whole, which is shorter than its diff:
```python
import jax
import jax.numpy as jnp
from jax import lax
from jax.experimental import pallas as pl
from jax.experimental.pallas import tpu as pltpu
from jax.sharding import PartitionSpec as P

MESH = pl.DeviceIdType.MESH
F32 = jnp.float32
BF16 = jnp.bfloat16
TEAMS = 8
GROUPS = 8
DEPTH = 80
ROWS = 256


def remote(src, dst, send_sem, recv_sem, day, pt):
    return pltpu.make_async_remote_copy(
        src_ref=src,
        dst_ref=dst,
        send_sem=send_sem,
        recv_sem=recv_sem,
        device_id=(day, pt),
        device_id_type=MESH,
    )


def parts_of(norm):
    first = norm.astype(BF16).astype(F32)
    rest = norm - first
    second = rest.astype(BF16).astype(F32)
    third = (rest - second).astype(BF16).astype(F32)
    return first, second, third


def fill_side(side, coords, factor, norms_first):
    wide = coords.astype(F32)
    norm = -jnp.sum(wide * wide, axis=0, keepdims=True)
    one, two, three = parts_of(norm)
    shape = (DEPTH - 64, coords.shape[1])
    row = lax.broadcasted_iota(jnp.int32, shape, 0)
    if not norms_first:
        row = jnp.where(row < 3, row + 3, jnp.where(row < 6, row - 3, row))
    extra = jnp.where(row == 0, one, jnp.where(row == 1, two, jnp.where(row == 2, three, 0.0)))
    extra = jnp.where((row >= 3) & (row < 6), 1.0, extra)
    side[0:64, :] = (wide * factor).astype(BF16)
    side[64:DEPTH, :] = extra.astype(BF16)


def body(
    pts_in, cells_in, cw_in, pot_in, sc_in, cc_in, fb_out, fit_out,
    kern, fit, pts, wts, res, oth, msg, wsrc, left, right, mps, mbuf, mrow, rpart, rbuf,
    rs_p, rs_w, ss_p, ss_w, ss_i, ss_f, ss_g, rs_u, ss_u, rs_o, ss_o, rs_x, ss_x, rs_m, ss_m,
    rs_r, ss_r,
):
    d = lax.axis_index("day")
    p = lax.axis_index("pt")
    q = d // 4
    dl = d % 4
    core = d % 2
    pair = q % 2
    xb = (d // 2) % 2
    bit = jnp.where(pair == 0, xb, 1 - xb)
    g = 2 * p + bit
    early = core == 1
    low = q < TEAMS // 2
    fwd = early == low
    stage = jnp.where(fwd, q, TEAMS - 1 - q)
    starts = stage == 0
    own_col = pl.multiple_of(p * 512, 512)

    def day_at(place):
        return 4 * q + jnp.where(fwd, place - 1, 4 - place)

    def chain_day(team, group, at_core):
        flip = team % 2
        side = group % 2
        return 4 * team + 2 * jnp.where(flip == 0, side, 1 - side) + at_core

    barrier = pltpu.get_barrier_semaphore()

    def greet(n, carry):
        team = q - 1 + n // 16
        day = 4 * team + (n % 16) // 4
        pt = n % 4
        ok = (team >= 0) & (team < TEAMS) & jnp.logical_not((day == d) & (pt == p))

        @pl.when(ok)
        def _():
            pl.semaphore_signal(barrier, inc=1, device_id=(day, pt), device_id_type=MESH)

        return carry

    lax.fori_loop(0, 48, greet, 0)

    slot_own = lax.broadcasted_iota(jnp.int32, (1, 512), 1) + p * 512
    live_own = (slot_own < sc_in[0]).astype(F32)
    wsrc[...] = cw_in[0] * (pot_in[...] * live_own)

    others = 15 + jnp.where(q > 0, 16, 0) + jnp.where(q < TEAMS - 1, 16, 0)
    pl.semaphore_wait(barrier, others)

    place_own = jnp.where(low, dl + 1, 4 - dl)

    def pts_copy(group, team, at_core, place, send_sem):
        return remote(
            pts_in.at[0],
            pts.at[place, :, pl.ds(own_col, 512)],
            send_sem,
            rs_p.at[place, p],
            chain_day(team, group, at_core),
            group // 2,
        )

    def wts_copy(group):
        return remote(
            wsrc.at[pl.ds(pl.multiple_of(8 * group, 8), 8), :],
            wts.at[place_own - 1, :, pl.ds(own_col, 512)],
            ss_w.at[group],
            rs_w.at[place_own - 1, p],
            chain_day(q, group, 1),
            group // 2,
        )

    def is_self(group):
        return (chain_day(q, group, 1) == d) & (group // 2 == p)

    def give(group, carry):
        @pl.when(is_self(group))
        def _():
            pltpu.make_async_copy(
                pts_in.at[0], pts.at[place_own, :, pl.ds(own_col, 512)], rs_p.at[place_own, p]
            ).start()
            pltpu.make_async_copy(
                wsrc.at[pl.ds(pl.multiple_of(8 * group, 8), 8), :],
                wts.at[place_own - 1, :, pl.ds(own_col, 512)],
                rs_w.at[place_own - 1, p],
            ).start()

        @pl.when(jnp.logical_not(is_self(group)))
        def _():
            pts_copy(group, q, 1, place_own, ss_p.at[group]).start()
            wts_copy(group).start()

        return carry

    lax.fori_loop(0, GROUPS, give, 0)

    to_next = (dl == 3) & (q < TEAMS - 1)
    to_last = (dl == 0) & (q > 0)
    side_team = jnp.where(dl == 3, q + 1, q - 1)
    side_core = jnp.where(
        dl == 3,
        jnp.where(side_team < TEAMS // 2, 1, 0),
        jnp.where(side_team < TEAMS // 2, 0, 1),
    )

    def side_copy(group):
        return pts_copy(group, side_team, side_core, 0, ss_i.at[group])

    @pl.when(to_next | to_last)
    def _():
        def give_side(group, carry):
            side_copy(group).start()
            return carry

        lax.fori_loop(0, GROUPS, give_side, 0)

    mate = d - 1

    def pts_pass(place):
        return remote(
            pts.at[place], pts.at[5 - place], ss_f.at[place - 1], rs_p.at[5 - place, 0], mate, p
        )

    def wts_pass(index):
        return remote(
            wts.at[index], wts.at[3 - index], ss_g.at[index], rs_w.at[3 - index, 0], mate, p
        )

    def wait_blocks(place):
        def one(k, carry):
            dst = pts.at[place, :, pl.ds(pl.multiple_of(k * 512, 512), 512)]
            remote(pts_in.at[0], dst, ss_u, rs_p.at[place, k], d, p).wait_recv()
            return carry

        lax.fori_loop(0, 4, one, 0)

    def take_day(place):
        @pl.when(early)
        def _():
            wait_blocks(place)
            pts_pass(place).start()

            def one(k, carry):
                dst = wts.at[place - 1, :, pl.ds(pl.multiple_of(k * 512, 512), 512)]
                src = wsrc.at[pl.ds(0, 8), :]
                remote(src, dst, ss_u, rs_w.at[place - 1, k], d, p).wait_recv()
                return carry

            lax.fori_loop(0, 4, one, 0)
            wts_pass(place - 1).start()

        @pl.when(jnp.logical_not(early))
        def _():
            remote(
                pts.at[place], pts.at[place], ss_u, rs_p.at[place, 0], d, p
            ).wait_recv()
            remote(
                wts.at[place - 1], wts.at[place - 1], ss_u, rs_w.at[place - 1, 0], d, p
            ).wait_recv()

    def send_form(values):
        return jnp.concatenate([values[:, 0:1024], values[:, 1024:2048]], axis=0).astype(BF16)

    def step(index):
        low_part = jnp.dot(msg[...], kern[index, 0:1024, :], preferred_element_type=F32)
        high_part = jnp.dot(msg[...], kern[index, 1024:2048, :], preferred_element_type=F32)
        weight = wts[index]
        live = (weight > 0.0).astype(F32)
        count = jnp.sum(live, axis=1, keepdims=True)
        masked = (low_part[0:8] + high_part[8:16]) * live
        settled = masked * (count / jnp.sum(masked, axis=1, keepdims=True))
        msg[...] = send_form(settled * weight)
        res[index] = settled

    take_day(1)

    @pl.when(starts)
    def _():
        weight = wts[0]
        live = (weight > 0.0).astype(F32)
        res[0] = live
        msg[...] = send_form(live * weight)

    def make_kernel(t, carry):
        index = (t + 1) % 4

        @pl.when(index > 0)
        def _():
            take_day(index + 1)

        @pl.when((index > 0) | jnp.logical_not(starts))
        def _():
            @pl.when(index == 0)
            def _():
                wait_blocks(0)

            fill_side(left, pts[index], 1.0, True)
            fill_side(right, pts[index + 1], 2.0, False)

            def rows(r, inner):
                at = pl.ds(pl.multiple_of(r * ROWS, ROWS), ROWS)
                power = lax.dot_general(
                    left[:, at], right[...], (((0,), (0,)), ((), ())), preferred_element_type=F32
                )
                kern[index, at, :] = jnp.exp(power).astype(BF16)
                return inner

            lax.fori_loop(0, 2048 // ROWS, rows, 0)

        @pl.when((index > 0) & starts)
        def _():
            step(index)

        return carry

    lax.fori_loop(0, 4, make_kernel, 0)

    def make_fit():
        fill_side(left, pts[jnp.where(fwd, dl + 1, 4 - dl)], 1.0, True)
        fill_side(right, cells_in[0], 2.0, False)

        def rows(r, inner):
            at = pl.ds(pl.multiple_of(r * ROWS, ROWS), ROWS)
            power = lax.dot_general(
                left[:, at], right[...], (((0,), (0,)), ((), ())), preferred_element_type=F32
            )
            fit[at, :] = jnp.exp(power)
            return inner

        lax.fori_loop(0, 2048 // ROWS, rows, 0)

    next_team = jnp.where(fwd, q + 1, q - 1)
    next_core = jnp.where(fwd == (next_team < TEAMS // 2), 1, 0)
    next_day = 4 * next_team + 2 * (1 - xb) + next_core
    hop = remote(msg, msg, ss_u, rs_u, next_day, p)

    def cross(index):
        return remote(res.at[index], oth.at[3 - index], ss_x.at[index], rs_x.at[3 - index], mate, p)

    @pl.when(jnp.logical_not(early))
    def _():
        make_fit()

    @pl.when(jnp.logical_not(starts))
    def _():
        remote(msg, msg, ss_u, rs_u, d, p).wait_recv()

        def one(index, carry):
            step(index)
            return carry

        lax.fori_loop(0, 4, one, 0)

    @pl.when(stage < TEAMS - 1)
    def _():
        hop.start()

    def mass_copy(index, k):
        return remote(
            mps.at[index], mbuf.at[g], ss_m.at[index, k], rs_m.at[g], day_at(index + 1), k
        )

    def here(index, k):
        return (day_at(index + 1) == d) & (k == p)

    @pl.when(jnp.logical_not(early))
    def _():
        def one(t, carry):
            index = 3 - t
            remote(res.at[index], oth.at[index], ss_u, rs_x.at[index], d, p).wait_recv()
            mps[index] = jnp.sum(res[index] * wts[index] * oth[index], axis=0, keepdims=True)

            def to(k, inner):
                @pl.when(here(index, k))
                def _():
                    pltpu.make_async_copy(mps.at[index], mbuf.at[g], rs_m.at[g]).start()

                @pl.when(jnp.logical_not(here(index, k)))
                def _():
                    mass_copy(index, k).start()

                return inner

            lax.fori_loop(0, 4, to, 0)
            return carry

        lax.fori_loop(0, 4, one, 0)

    @pl.when(early)
    def _():
        def one(index, carry):
            cross(index).start()
            return carry

        lax.fori_loop(0, 4, one, 0)

    way = jnp.where(fwd, 0, 1)
    rows_g = pl.ds(pl.multiple_of(8 * g, 8), 8)

    def out_copy(index, k):
        return remote(
            res.at[index, :, pl.ds(pl.multiple_of(k * 512, 512), 512)],
            fb_out.at[way, rows_g, :],
            ss_o.at[index, k],
            rs_o.at[way, g],
            day_at(index + 1),
            k,
        )

    def out_days(index, carry):
        def to(k, inner):
            @pl.when(here(index, k))
            def _():
                pltpu.make_async_copy(
                    res.at[index, :, pl.ds(pl.multiple_of(k * 512, 512), 512)],
                    fb_out.at[way, rows_g, :],
                    rs_o.at[way, g],
                ).start()

            @pl.when(jnp.logical_not(here(index, k)))
            def _():
                out_copy(index, k).start()

            return inner

        lax.fori_loop(0, 4, to, 0)
        return carry

    lax.fori_loop(0, 4, out_days, 0)

    @pl.when(early)
    def _():
        make_fit()

    def wait_mass(k, carry):
        remote(mps.at[0], mbuf.at[k], ss_u, rs_m.at[k], d, p).wait_recv()
        return carry

    lax.fori_loop(0, GROUPS, wait_mass, 0)
    mass = mbuf[0]
    for k in range(1, GROUPS):
        mass = mass + mbuf[k]
    mass_total = jnp.sum(mass, axis=1, keepdims=True)
    mrow[...] = jnp.zeros_like(mrow)
    for k in range(16):
        mrow[k : k + 1, :] = mass[:, 128 * k : 128 * k + 128]
    columns = jnp.transpose(mrow[...])
    total = jnp.zeros((8, 2048), F32)
    for k in range(16):
        block = fit[128 * k : 128 * k + 128, :] * columns[:, k : k + 1]
        total = total + jnp.sum(block.reshape(16, 8, 2048), axis=0)
    density = jnp.sum(total, axis=0, keepdims=True) / mass_total
    cell = lax.broadcasted_iota(jnp.int32, (1, 2048), 1) + p * 2048
    inverse = (cell < cc_in[0]).astype(F32) / density
    for k in range(16):
        part = jnp.zeros((128, 128), F32)
        for c in range(16):
            part = part + (
                fit[128 * k : 128 * k + 128, 128 * c : 128 * c + 128]
                * inverse[:, 128 * c : 128 * c + 128]
            )
        rpart[k // 4, :, 128 * (k % 4) : 128 * (k % 4) + 128] = jnp.sum(
            jnp.transpose(part), axis=0, keepdims=True
        )

    def ratio_copy(k):
        return remote(rpart.at[k], rbuf.at[p], ss_r.at[k], rs_r.at[p], d, k)

    def ratio_to(k, carry):
        @pl.when(k == p)
        def _():
            pltpu.make_async_copy(rpart.at[k], rbuf.at[p], rs_r.at[p]).start()

        @pl.when(k != p)
        def _():
            ratio_copy(k).start()

        return carry

    lax.fori_loop(0, 4, ratio_to, 0)

    def ratio_wait(k, carry):
        remote(rpart.at[0], rbuf.at[k], ss_u, rs_r.at[k], d, p).wait_recv()
        return carry

    lax.fori_loop(0, 4, ratio_wait, 0)
    summed = rbuf[0] + rbuf[1] + rbuf[2] + rbuf[3]
    fit_out[...] = live_own / jnp.full((1, 512), cc_in[0], jnp.int32).astype(F32) * summed

    def close_give(group, carry):
        @pl.when(jnp.logical_not(is_self(group)))
        def _():
            pts_copy(group, q, 1, place_own, ss_p.at[group]).wait_send()
            wts_copy(group).wait_send()

        @pl.when(to_next | to_last)
        def _():
            side_copy(group).wait_send()

        def arrived(way_in, inner):
            remote(
                res.at[0, :, pl.ds(0, 512)],
                fb_out.at[way_in, pl.ds(pl.multiple_of(8 * group, 8), 8), :],
                ss_u,
                rs_o.at[way_in, group],
                d,
                p,
            ).wait_recv()
            return inner

        lax.fori_loop(0, 2, arrived, 0)
        return carry

    lax.fori_loop(0, GROUPS, close_give, 0)

    def close_four(index, carry):
        @pl.when(early)
        def _():
            pts_pass(index + 1).wait_send()
            wts_pass(index).wait_send()
            cross(index).wait_send()

        @pl.when(index != p)
        def _():
            ratio_copy(index).wait_send()

        def to(k, inner):
            @pl.when(jnp.logical_not(here(index, k)))
            def _():
                out_copy(index, k).wait_send()

                @pl.when(jnp.logical_not(early))
                def _():
                    mass_copy(index, k).wait_send()

            return inner

        lax.fori_loop(0, 4, to, 0)
        return carry

    lax.fori_loop(0, 4, close_four, 0)

    @pl.when(stage < TEAMS - 1)
    def _():
        hop.wait_send()


def shards(points, cells, clone_weight, potential, support_count, cell_count):
    vmem = pl.BlockSpec(memory_space=pltpu.VMEM)
    smem = pl.BlockSpec(memory_space=pltpu.SMEM)
    dma = pltpu.SemaphoreType.DMA
    both, ratio = pl.pallas_call(
        body,
        out_shape=(
            jax.ShapeDtypeStruct((2, 64, 512), F32),
            jax.ShapeDtypeStruct((1, 512), F32),
        ),
        in_specs=[vmem, vmem, vmem, vmem, smem, smem],
        out_specs=(pl.BlockSpec(memory_space=pl.ANY), vmem),
        scratch_shapes=[
            pltpu.VMEM((4, 2048, 2048), BF16),
            pltpu.VMEM((2048, 2048), F32),
            pltpu.VMEM((5, 64, 2048), BF16),
            pltpu.VMEM((4, 8, 2048), F32),
            pltpu.VMEM((4, 8, 2048), F32),
            pltpu.VMEM((4, 8, 2048), F32),
            pltpu.VMEM((16, 1024), BF16),
            pltpu.VMEM((64, 512), F32),
            pltpu.VMEM((DEPTH, 2048), BF16),
            pltpu.VMEM((DEPTH, 2048), BF16),
            pltpu.VMEM((4, 1, 2048), F32),
            pltpu.VMEM((GROUPS, 1, 2048), F32),
            pltpu.VMEM((128, 128), F32),
            pltpu.VMEM((4, 1, 512), F32),
            pltpu.VMEM((4, 1, 512), F32),
            dma((5, 4)),
            dma((4, 4)),
            dma((GROUPS,)),
            dma((GROUPS,)),
            dma((GROUPS,)),
            dma((4,)),
            dma((4,)),
            dma,
            dma,
            dma((2, GROUPS)),
            dma((4, 4)),
            dma((4,)),
            dma((4,)),
            dma((GROUPS,)),
            dma((4, 4)),
            dma((4,)),
            dma((4,)),
        ],
        compiler_params=pltpu.CompilerParams(
            collective_id=0, has_side_effects=True, vmem_limit_bytes=58 * 1024 * 1024
        ),
        name="days",
    )(points, cells, clone_weight, potential, support_count, cell_count)
    return both[0][None], both[1][None], ratio


def solution(mesh):
    in_specs = (
        P("day", None, "pt"),
        P("day", None, "pt"),
        P("day", None, "pt"),
        P("day", "pt"),
        P("day"),
        P("day"),
    )
    out_specs = (P("day", None, "pt"), P("day", None, "pt"), P("day", "pt"))
    return jax.shard_map(shards, mesh=mesh, in_specs=in_specs, out_specs=out_specs, check_vma=False)
```

time: 1620 us -> 115 us (0.07)
  blocking collectives: 689 us -> 0 us
  starting transfers between devices: 526 us -> 0 us
  waiting for transfers between devices: 121 us -> 0 us
  matrix products: 119 us -> 0 us
  Pallas kernels: 0 us -> 110 us
  other arithmetic: 65.8 us -> 0 us
  local copies, waits for them, and re-layouts: 55.5 us -> 2.94 us
    all_gather x73 -> x0, blocking collectives: 675 us -> none  [the longest x35 322 us: one_step(): lax.all_gather(forward_piece, 'pt', axis=1, tiled=True)]
    ppermute x72 -> x0, starting transfers between devices: 526 us -> none  [the longest x70 517 us: shifted(): return lax.ppermute(block, axis, route)]
    ppermute x72 -> x0, waiting for transfers between devices: 121 us -> none  [the longest x70 121 us: shifted(): return lax.ppermute(block, axis, route)]
    dot_general x96 -> x0, matrix products: 119 us -> none  [the longest x32 53.9 us: add_rows(): jnp.dot(sent_part, kernel_rows(source_pts, source_norm, block_index), pre...]
    pallas_call x0 -> x1, Pallas kernels: none -> 110 us  [shards(): pl.pallas_call(body, out_shape=(jax.ShapeDtypeStruct((2, 64, 512), F32),...]
    another operation x62 -> x0, local copies, waits for them, and re-layouts: 38.3 us -> none
    select_n x105 -> x0, other arithmetic: 30.7 us -> none  [the longest x35 27.4 us: one_step(): jnp.where(day_index == day_count - 1, seed_rows, backward_got)]
    convert_element_type x71 -> x0, other arithmetic: 26.3 us -> none  [the longest x36 22.7 us: shards(): (jnp.arange(support_total, dtype=jnp.int32) < support_count[0]).astype(jn...]
  transfers between devices with their start and end apart: 73 -> 0, of which waited for: 35 -> 0; matrix products, arithmetic and copies ran while one was open for 10% -> 0% of each run, Pallas kernels for 0% -> 0%
where the time goes in v1:
time: 115 us
  Pallas kernels  110 us (96%)
  local copies, waits for them, and re-layouts  2.94 us (3%)
  between operations  1.93 us (2%)
    pallas_call x1, Pallas kernels, shards(): pl.pallas_call(body, out_shape=(jax.ShapeDtypeStruct((2, 64, 512), F32),...  110 us

profile of v1, /device:TPU:1, one launch (start us, length us, event | category | flops | bytes accessed | tf_op | source)
XLA Modules:
  0.0 114.9 jit_solution(2665187549119252520)
XLA Ops:
  1.9 110.1 %days.1 = (f32[2,64,512]{2,1,0:T(8,128)}, f32[1,512]{1,0:T(1,128)}) custom-call(bf16[1,64,512]{2,1,0:T(8,128)(2,1)} %pts_in.1, bf16[1,64,2048]{2,1,0:T(8,128)(2,1)} %cells_in.1, f32[1,64,512]{2,1,0:T(8,128)} %cw_in.1, f32[1,512]{1,0:T(1,128)} %pot_in.1, s32[1]{0:T(128)S(6)} %copy.10.sc_in, s32[1]{0:T(128)S(6)} %copy.11.cc_in), custom_call_target="tpu_custom_call" | custom-call | tf_op jit(solution)/shard_map/days/pallas_call | solution.py:504
  112.0 1.7 %fusion = (f32[1,64,512]{2,1,0:T(8,128)}, f32[1,64,512]{2,1,0:T(8,128)}) fusion(f32[2,64,512]{2,1,0:T(8,128)} %get-tuple-element.5), kind=kLoop, calls=%fused_computation | loop fusion | bytes 524288 | tf_op jit(solution)/shard_map/slice | solution.py:551
  113.7 0.0 copy-start
  113.7 0.7 copy-done
  114.4 0.6 copy.12
Async XLA Ops:
  113.7 0.7 copy-start

commit v2 on v1

--- a/solution.py
+++ b/solution.py
@@ -11,7 +11,8 @@
 TEAMS = 8
 GROUPS = 8
 DEPTH = 80
-ROWS = 256
+ROWS = 512
+ROWS_SUMMED = 512
 
 
 def remote(src, dst, send_sem, recv_sem, day, pt):
@@ -49,7 +50,7 @@
 
 def body(
     pts_in, cells_in, cw_in, pot_in, sc_in, cc_in, fb_out, fit_out,
-    kern, fit, pts, wts, res, oth, msg, wsrc, left, right, mps, mbuf, mrow, rpart, rbuf,
+    kern, rsum, fit, pts, wts, res, oth, msg, wsrc, left, right, mps, mbuf, mrow, rpart, rbuf,
     rs_p, rs_w, ss_p, ss_w, ss_i, ss_f, ss_g, rs_u, ss_u, rs_o, ss_o, rs_x, ss_x, rs_m, ss_m,
     rs_r, ss_r,
 ):
@@ -80,24 +81,38 @@
     barrier = pltpu.get_barrier_semaphore()
 
     def greet(n, carry):
-        team = q - 1 + n // 16
-        day = 4 * team + (n % 16) // 4
+        day = 4 * q + n // 4
         pt = n % 4
-        ok = (team >= 0) & (team < TEAMS) & jnp.logical_not((day == d) & (pt == p))
-
-        @pl.when(ok)
+
+        @pl.when(jnp.logical_not((day == d) & (pt == p)))
         def _():
             pl.semaphore_signal(barrier, inc=1, device_id=(day, pt), device_id_type=MESH)
 
         return carry
 
-    lax.fori_loop(0, 48, greet, 0)
+    lax.fori_loop(0, 16, greet, 0)
+
+    @pl.when(jnp.logical_not(starts))
+    def _():
+        last_team = jnp.where(fwd, q - 1, q + 1)
+        last_core = jnp.where(fwd == (last_team < TEAMS // 2), 1, 0)
+        last_day = 4 * last_team + 2 * (1 - xb) + last_core
+        pl.semaphore_signal(barrier, inc=1, device_id=(last_day, p), device_id_type=MESH)
+
+        def greet_side(pt, carry):
+            day = jnp.where(fwd, 4 * q - 1, 4 * q + 4)
+            pl.semaphore_signal(barrier, inc=1, device_id=(day, pt), device_id_type=MESH)
+            return carry
+
+        lax.fori_loop(0, 4, greet_side, 0)
 
     slot_own = lax.broadcasted_iota(jnp.int32, (1, 512), 1) + p * 512
     live_own = (slot_own < sc_in[0]).astype(F32)
     wsrc[...] = cw_in[0] * (pot_in[...] * live_own)
 
-    others = 15 + jnp.where(q > 0, 16, 0) + jnp.where(q < TEAMS - 1, 16, 0)
+    to_next = (dl == 3) & (q < TEAMS - 1)
+    to_last = (dl == 0) & (q > 0)
+    others = 15 + jnp.where(to_next | to_last, GROUPS, 0) + jnp.where(stage < TEAMS - 1, 1, 0)
     pl.semaphore_wait(barrier, others)
 
     place_own = jnp.where(low, dl + 1, 4 - dl)
@@ -125,12 +140,22 @@
     def is_self(group):
         return (chain_day(q, group, 1) == d) & (group // 2 == p)
 
-    def give(group, carry):
+    def give_pts(group, carry):
         @pl.when(is_self(group))
         def _():
             pltpu.make_async_copy(
                 pts_in.at[0], pts.at[place_own, :, pl.ds(own_col, 512)], rs_p.at[place_own, p]
             ).start()
+
+        @pl.when(jnp.logical_not(is_self(group)))
+        def _():
+            pts_copy(group, q, 1, place_own, ss_p.at[group]).start()
+
+        return carry
+
+    def give_wts(group, carry):
+        @pl.when(is_self(group))
+        def _():
             pltpu.make_async_copy(
                 wsrc.at[pl.ds(pl.multiple_of(8 * group, 8), 8), :],
                 wts.at[place_own - 1, :, pl.ds(own_col, 512)],
@@ -139,15 +164,19 @@
 
         @pl.when(jnp.logical_not(is_self(group)))
         def _():
-            pts_copy(group, q, 1, place_own, ss_p.at[group]).start()
             wts_copy(group).start()
 
         return carry
 
-    lax.fori_loop(0, GROUPS, give, 0)
-
-    to_next = (dl == 3) & (q < TEAMS - 1)
-    to_last = (dl == 0) & (q > 0)
+    def give():
+        def turned(group):
+            return lax.rem(group + 2 * p + 2, GROUPS)
+
+        lax.fori_loop(0, GROUPS, lambda n, carry: give_pts(turned(n), carry), 0)
+        lax.fori_loop(0, GROUPS, lambda n, carry: give_wts(turned(n), carry), 0)
+
+    give()
+
     side_team = jnp.where(dl == 3, q + 1, q - 1)
     side_core = jnp.where(
         dl == 3,
@@ -158,14 +187,6 @@
     def side_copy(group):
         return pts_copy(group, side_team, side_core, 0, ss_i.at[group])
 
-    @pl.when(to_next | to_last)
-    def _():
-        def give_side(group, carry):
-            side_copy(group).start()
-            return carry
-
-        lax.fori_loop(0, GROUPS, give_side, 0)
-
     mate = d - 1
 
     def pts_pass(place):
@@ -186,63 +207,100 @@
 
         lax.fori_loop(0, 4, one, 0)
 
-    def take_day(place):
+    def take_pts(n):
         @pl.when(early)
         def _():
-            wait_blocks(place)
-            pts_pass(place).start()
-
+            wait_blocks(n)
+            pts_pass(n).start()
+
+        @pl.when(jnp.logical_not(early))
+        def _():
+            place = 5 - n
+            remote(pts.at[place], pts.at[place], ss_u, rs_p.at[place, 0], d, p).wait_recv()
+
+    def take_wts(n):
+        @pl.when(early)
+        def _():
             def one(k, carry):
-                dst = wts.at[place - 1, :, pl.ds(pl.multiple_of(k * 512, 512), 512)]
+                dst = wts.at[n - 1, :, pl.ds(pl.multiple_of(k * 512, 512), 512)]
                 src = wsrc.at[pl.ds(0, 8), :]
-                remote(src, dst, ss_u, rs_w.at[place - 1, k], d, p).wait_recv()
+                remote(src, dst, ss_u, rs_w.at[n - 1, k], d, p).wait_recv()
                 return carry
 
             lax.fori_loop(0, 4, one, 0)
-            wts_pass(place - 1).start()
+            wts_pass(n - 1).start()
 
         @pl.when(jnp.logical_not(early))
         def _():
-            remote(
-                pts.at[place], pts.at[place], ss_u, rs_p.at[place, 0], d, p
-            ).wait_recv()
-            remote(
-                wts.at[place - 1], wts.at[place - 1], ss_u, rs_w.at[place - 1, 0], d, p
-            ).wait_recv()
+            index = 4 - n
+            remote(wts.at[index], wts.at[index], ss_u, rs_w.at[index, 0], d, p).wait_recv()
 
     def send_form(values):
         return jnp.concatenate([values[:, 0:1024], values[:, 1024:2048]], axis=0).astype(BF16)
 
-    def step(index):
-        low_part = jnp.dot(msg[...], kern[index, 0:1024, :], preferred_element_type=F32)
-        high_part = jnp.dot(msg[...], kern[index, 1024:2048, :], preferred_element_type=F32)
+    def advance(sent, index, sums):
         weight = wts[index]
         live = (weight > 0.0).astype(F32)
         count = jnp.sum(live, axis=1, keepdims=True)
-        masked = (low_part[0:8] + high_part[8:16]) * live
-        settled = masked * (count / jnp.sum(masked, axis=1, keepdims=True))
-        msg[...] = send_form(settled * weight)
-        res[index] = settled
-
-    take_day(1)
-
-    @pl.when(starts)
-    def _():
-        weight = wts[0]
-        live = (weight > 0.0).astype(F32)
-        res[0] = live
-        msg[...] = send_form(live * weight)
+        if sums:
+            row = rsum[index]
+            each = jnp.concatenate(
+                [
+                    jnp.sum(sent[0:8].astype(F32) * row[:, 0:1024], axis=1, keepdims=True),
+                    jnp.sum(sent[8:16].astype(F32) * row[:, 1024:2048], axis=1, keepdims=True),
+                ],
+                axis=0,
+            )
+            scale = count / (each[0:8] + each[8:16])
+            scaled = live * scale
+        out = []
+        for n in range(4):
+            at = slice(512 * n, 512 * n + 512)
+            low_part = jnp.dot(sent, kern[index, 0:1024, at], preferred_element_type=F32)
+            high_part = jnp.dot(sent, kern[index, 1024:2048, at], preferred_element_type=F32)
+            got = low_part[0:8] + high_part[8:16]
+            out.append(got * (scaled if sums else live)[:, at])
+        if not sums:
+            scale = count / sum(jnp.sum(part, axis=1, keepdims=True) for part in out)
+            out = [part * scale for part in out]
+        for n in range(4):
+            res[index, :, 512 * n : 512 * n + 512] = out[n]
+            out[n] = out[n] * weight[:, 512 * n : 512 * n + 512]
+        return jnp.concatenate(
+            [jnp.concatenate([out[n], out[n + 2]], axis=0).astype(BF16) for n in range(2)], axis=1
+        )
+
+    take_pts(1)
+    take_pts(2)
+
+    @pl.when(to_next | to_last)
+    def _():
+        def give_side(group, carry):
+            side_copy(group).start()
+            return carry
+
+        lax.fori_loop(0, GROUPS, give_side, 0)
+
+    quick = stage <= 1
 
     def make_kernel(t, carry):
-        index = (t + 1) % 4
-
-        @pl.when(index > 0)
-        def _():
-            take_day(index + 1)
-
-        @pl.when((index > 0) | jnp.logical_not(starts))
-        def _():
-            @pl.when(index == 0)
+        index = jnp.where(t == 3, 0, jnp.where(early, t + 1, 3 - t))
+
+        @pl.when((t == 1) | (t == 2))
+        def _():
+            take_pts(t + 2)
+
+        @pl.when(jnp.logical_not(starts) & (t == 0))
+        def _():
+            take_wts(1)
+
+        @pl.when(jnp.logical_not(starts) & (t < 3))
+        def _():
+            take_wts(t + 2)
+
+        @pl.when((t < 3) | jnp.logical_not(starts))
+        def _():
+            @pl.when(t == 3)
             def _():
                 wait_blocks(0)
 
@@ -254,14 +312,51 @@
                 power = lax.dot_general(
                     left[:, at], right[...], (((0,), (0,)), ((), ())), preferred_element_type=F32
                 )
-                kern[index, at, :] = jnp.exp(power).astype(BF16)
+                values = jnp.exp(power).astype(BF16)
+                kern[index, at, :] = values
                 return inner
 
-            lax.fori_loop(0, 2048 // ROWS, rows, 0)
-
-        @pl.when((index > 0) & starts)
-        def _():
-            step(index)
+            def rows_summed(r, inner):
+                at = pl.ds(pl.multiple_of(r * ROWS_SUMMED, ROWS_SUMMED), ROWS_SUMMED)
+                power = lax.dot_general(
+                    left[:, at], right[...], (((0,), (0,)), ((), ())), preferred_element_type=F32
+                )
+                values = jnp.exp(power).astype(BF16)
+                kern[index, at, :] = values
+                live = (wts[index, 0:1, :] > 0.0).astype(F32)
+                part = jnp.zeros((ROWS_SUMMED, 128), F32)
+                for c in range(16):
+                    cut = slice(128 * c, 128 * c + 128)
+                    part = part + values[:, cut].astype(F32) * live[:, cut]
+                rsum[index, :, at] = jnp.concatenate(
+                    [
+                        jnp.sum(jnp.transpose(part[128 * c : 128 * c + 128]), axis=0, keepdims=True)
+                        for c in range(ROWS_SUMMED // 128)
+                    ],
+                    axis=1,
+                )
+                return inner
+
+            @pl.when(quick)
+            def _():
+                lax.fori_loop(0, 2048 // ROWS, rows, 0)
+
+            @pl.when(jnp.logical_not(quick))
+            def _():
+                lax.fori_loop(0, 2048 // ROWS_SUMMED, rows_summed, 0)
+
+        @pl.when(starts & (t == 0))
+        def _():
+            take_wts(1)
+            weight = wts[0]
+            live = (weight > 0.0).astype(F32)
+            res[0] = live
+            msg[...] = send_form(live * weight)
+
+        @pl.when(starts & (t < 3))
+        def _():
+            take_wts(t + 2)
+            msg[...] = advance(msg[...], index, False)
 
         return carry
 
@@ -272,14 +367,14 @@
         fill_side(right, cells_in[0], 2.0, False)
 
         def rows(r, inner):
-            at = pl.ds(pl.multiple_of(r * ROWS, ROWS), ROWS)
+            at = pl.ds(pl.multiple_of(r * ROWS_SUMMED, ROWS_SUMMED), ROWS_SUMMED)
             power = lax.dot_general(
                 left[:, at], right[...], (((0,), (0,)), ((), ())), preferred_element_type=F32
             )
             fit[at, :] = jnp.exp(power)
             return inner
 
-        lax.fori_loop(0, 2048 // ROWS, rows, 0)
+        lax.fori_loop(0, 2048 // ROWS_SUMMED, rows, 0)
 
     next_team = jnp.where(fwd, q + 1, q - 1)
     next_core = jnp.where(fwd == (next_team < TEAMS // 2), 1, 0)
@@ -297,11 +392,20 @@
     def _():
         remote(msg, msg, ss_u, rs_u, d, p).wait_recv()
 
-        def one(index, carry):
-            step(index)
-            return carry
-
-        lax.fori_loop(0, 4, one, 0)
+        @pl.when(quick)
+        def _():
+            def one(index, carry):
+                msg[...] = advance(msg[...], index, False)
+                return carry
+
+            lax.fori_loop(0, 4, one, 0)
+
+        @pl.when(jnp.logical_not(quick))
+        def _():
+            sent = msg[...]
+            for index in range(4):
+                sent = advance(sent, index, True)
+            msg[...] = sent
 
     @pl.when(stage < TEAMS - 1)
     def _():
@@ -511,6 +615,7 @@
         out_specs=(pl.BlockSpec(memory_space=pl.ANY), vmem),
         scratch_shapes=[
             pltpu.VMEM((4, 2048, 2048), BF16),
+            pltpu.VMEM((4, 1, 2048), F32),
             pltpu.VMEM((2048, 2048), F32),
             pltpu.VMEM((5, 64, 2048), BF16),
             pltpu.VMEM((4, 8, 2048), F32),
@@ -544,7 +649,7 @@
             dma((4,)),
         ],
         compiler_params=pltpu.CompilerParams(
-            collective_id=0, has_side_effects=True, vmem_limit_bytes=58 * 1024 * 1024
+            collective_id=0, has_side_effects=True, vmem_limit_bytes=62 * 1024 * 1024
         ),
         name="days",
     )(points, cells, clone_weight, potential, support_count, cell_count)

time: 115 us -> 102 us (0.89)
  Pallas kernels: 110 us -> 97.3 us
    pallas_call x1, Pallas kernels: 110 us -> 97.3 us  [shards(): pl.pallas_call(body, out_shape=(jax.ShapeDtypeStruct((2, 64, 512), F32),...]
where the time goes in v2:
time: 102 us
  Pallas kernels  97.3 us (95%)
  local copies, waits for them, and re-layouts  2.94 us (3%)
  between operations  1.93 us (2%)
    pallas_call x1, Pallas kernels, shards(): pl.pallas_call(body, out_shape=(jax.ShapeDtypeStruct((2, 64, 512), F32),...  97.3 us

profile of v2, /device:TPU:1, one launch (start us, length us, event | category | flops | bytes accessed | tf_op | source)
XLA Modules:
  0.0 102.2 jit_solution(3228437384926705489)
XLA Ops:
  1.9 97.3 %days.1 = (f32[2,64,512]{2,1,0:T(8,128)}, f32[1,512]{1,0:T(1,128)}) custom-call(bf16[1,64,512]{2,1,0:T(8,128)(2,1)} %pts_in.1, bf16[1,64,2048]{2,1,0:T(8,128)(2,1)} %cells_in.1, f32[1,64,512]{2,1,0:T(8,128)} %cw_in.1, f32[1,512]{1,0:T(1,128)} %pot_in.1, s32[1]{0:T(128)S(6)} %copy.10.sc_in, s32[1]{0:T(128)S(6)} %copy.11.cc_in), custom_call_target="tpu_custom_call" | custom-call | tf_op jit(solution)/shard_map/days/pallas_call | solution.py:608
  99.3 1.7 %fusion = (f32[1,64,512]{2,1,0:T(8,128)}, f32[1,64,512]{2,1,0:T(8,128)}) fusion(f32[2,64,512]{2,1,0:T(8,128)} %get-tuple-element.5), kind=kLoop, calls=%fused_computation | loop fusion | bytes 524288 | tf_op jit(solution)/shard_map/slice | solution.py:656
  101.0 0.0 copy-start
  101.0 0.7 copy-done
  101.6 0.6 copy.12
Async XLA Ops:
  101.0 0.7 copy-start

commit v3 on v2

--- a/solution.py
+++ b/solution.py
@@ -11,7 +11,8 @@
 TEAMS = 8
 GROUPS = 8
 DEPTH = 80
-ROWS = 512
+ROWS = 2048
+PART = 512
 ROWS_SUMMED = 512
 
 
@@ -50,9 +51,9 @@
 
 def body(
     pts_in, cells_in, cw_in, pot_in, sc_in, cc_in, fb_out, fit_out,
-    kern, rsum, fit, pts, wts, res, oth, msg, wsrc, left, right, mps, mbuf, mrow, rpart, rbuf,
+    kern, rsum, fit, pts, wts, res, oth, msg, alt, turn, wsrc, left, right, mps, mbuf, mrow, rpart, rbuf,
     rs_p, rs_w, ss_p, ss_w, ss_i, ss_f, ss_g, rs_u, ss_u, rs_o, ss_o, rs_x, ss_x, rs_m, ss_m,
-    rs_r, ss_r,
+    rs_r, ss_r, rs_h, ss_h, rs_k, ss_k,
 ):
     d = lax.axis_index("day")
     p = lax.axis_index("pt")
@@ -238,8 +239,9 @@
     def send_form(values):
         return jnp.concatenate([values[:, 0:1024], values[:, 1024:2048]], axis=0).astype(BF16)
 
-    def advance(sent, index, sums):
-        weight = wts[index]
+    def advance(sent, index, sums, place=None):
+        place = index if place is None else place
+        weight = wts[place]
         live = (weight > 0.0).astype(F32)
         count = jnp.sum(live, axis=1, keepdims=True)
         if sums:
@@ -264,7 +266,7 @@
             scale = count / sum(jnp.sum(part, axis=1, keepdims=True) for part in out)
             out = [part * scale for part in out]
         for n in range(4):
-            res[index, :, 512 * n : 512 * n + 512] = out[n]
+            res[place, :, 512 * n : 512 * n + 512] = out[n]
             out[n] = out[n] * weight[:, 512 * n : 512 * n + 512]
         return jnp.concatenate(
             [jnp.concatenate([out[n], out[n + 2]], axis=0).astype(BF16) for n in range(2)], axis=1
@@ -282,38 +284,54 @@
         lax.fori_loop(0, GROUPS, give_side, 0)
 
     quick = stage <= 1
+    helps = stage == TEAMS - 1
+    ask = remote(msg, alt, ss_h, rs_h, mate, p)
+    reply = remote(turn, alt, ss_h, rs_h, d + 1, p)
+    reply_res = remote(res.at[1], res.at[2], ss_k, rs_k, d + 1, p)
 
     def make_kernel(t, carry):
-        index = jnp.where(t == 3, 0, jnp.where(early, t + 1, 3 - t))
-
-        @pl.when((t == 1) | (t == 2))
+        index = jnp.where((t == 3) | (t < 0), 0, jnp.where(early, t + 1, 3 - t))
+
+        first = t < 0
+        paired = starts | helps
+
+        @pl.when(((t == 1) & jnp.logical_not(paired)) | (t == 2))
         def _():
             take_pts(t + 2)
 
-        @pl.when(jnp.logical_not(starts) & (t == 0))
+        @pl.when(jnp.logical_not(paired) & (t == 0))
         def _():
             take_wts(1)
 
-        @pl.when(jnp.logical_not(starts) & (t < 3))
+        @pl.when((jnp.logical_not(paired) & (t < 3)) | (helps & (t == 2)))
         def _():
             take_wts(t + 2)
 
-        @pl.when((t < 3) | jnp.logical_not(starts))
+        @pl.when(first)
+        def _():
+            take_pts(3)
+            for n in range(1, 4):
+                take_wts(n)
+
+        @pl.when(jnp.logical_not(starts) | (t == 0) | (t == 2))
         def _():
             @pl.when(t == 3)
             def _():
                 wait_blocks(0)
 
-            fill_side(left, pts[index], 1.0, True)
-            fill_side(right, pts[index + 1], 2.0, False)
+            fill_side(left, pts[jnp.where(first, 3, index)], 1.0, True)
+            fill_side(right, pts[jnp.where(first, 2, index + 1)], 2.0, False)
 
             def rows(r, inner):
-                at = pl.ds(pl.multiple_of(r * ROWS, ROWS), ROWS)
-                power = lax.dot_general(
-                    left[:, at], right[...], (((0,), (0,)), ((), ())), preferred_element_type=F32
-                )
-                values = jnp.exp(power).astype(BF16)
-                kern[index, at, :] = values
+                for c in range(ROWS // PART):
+                    at = pl.ds(pl.multiple_of(r * ROWS + PART * c, PART), PART)
+                    power = lax.dot_general(
+                        left[:, at],
+                        right[...],
+                        (((0,), (0,)), ((), ())),
+                        preferred_element_type=F32,
+                    )
+                    kern[index, at, :] = jnp.exp(power).astype(BF16)
                 return inner
 
             def rows_summed(r, inner):
@@ -337,30 +355,58 @@
                 )
                 return inner
 
-            @pl.when(quick)
+            @pl.when(quick | first)
             def _():
                 lax.fori_loop(0, 2048 // ROWS, rows, 0)
 
-            @pl.when(jnp.logical_not(quick))
+            @pl.when(jnp.logical_not(quick | first))
             def _():
                 lax.fori_loop(0, 2048 // ROWS_SUMMED, rows_summed, 0)
 
         @pl.when(starts & (t == 0))
         def _():
-            take_wts(1)
+            take_pts(3)
+            for n in range(1, 4):
+                take_wts(n)
             weight = wts[0]
             live = (weight > 0.0).astype(F32)
             res[0] = live
             msg[...] = send_form(live * weight)
 
-        @pl.when(starts & (t < 3))
-        def _():
-            take_wts(t + 2)
-            msg[...] = advance(msg[...], index, False)
-
-        return carry
-
-    lax.fori_loop(0, 4, make_kernel, 0)
+        @pl.when(starts & (t == 2))
+        def _():
+            take_wts(4)
+            ask.wait_send()
+            ask.wait_recv()
+            reply_res.wait_recv()
+            msg[...] = alt[...]
+
+        @pl.when(first)
+        def _():
+            ask.wait_recv()
+            turn[...] = alt[...]
+
+        @pl.when((starts & ((t == 0) | (t == 2))) | first)
+        def _():
+            @pl.when(first)
+            def _():
+                turn[...] = advance(turn[...], 0, False, 1)
+                reply.start()
+                reply_res.start()
+                reply.wait_send()
+                reply_res.wait_send()
+
+            @pl.when(starts)
+            def _():
+                msg[...] = advance(msg[...], index, False)
+
+            @pl.when(starts & (t == 0))
+            def _():
+                ask.start()
+
+        return carry
+
+    lax.fori_loop(jnp.where(helps, -1, 0), 4, make_kernel, 0)
 
     def make_fit():
         fill_side(left, pts[jnp.where(fwd, dl + 1, 4 - dl)], 1.0, True)
@@ -535,14 +581,6 @@
 
     lax.fori_loop(0, 4, ratio_to, 0)
 
-    def ratio_wait(k, carry):
-        remote(rpart.at[0], rbuf.at[k], ss_u, rs_r.at[k], d, p).wait_recv()
-        return carry
-
-    lax.fori_loop(0, 4, ratio_wait, 0)
-    summed = rbuf[0] + rbuf[1] + rbuf[2] + rbuf[3]
-    fit_out[...] = live_own / jnp.full((1, 512), cc_in[0], jnp.int32).astype(F32) * summed
-
     def close_give(group, carry):
         @pl.when(jnp.logical_not(is_self(group)))
         def _():
@@ -576,10 +614,6 @@
             wts_pass(index).wait_send()
             cross(index).wait_send()
 
-        @pl.when(index != p)
-        def _():
-            ratio_copy(index).wait_send()
-
         def to(k, inner):
             @pl.when(jnp.logical_not(here(index, k)))
             def _():
@@ -599,6 +633,23 @@
     @pl.when(stage < TEAMS - 1)
     def _():
         hop.wait_send()
+
+    def ratio_wait(k, carry):
+        remote(rpart.at[0], rbuf.at[k], ss_u, rs_r.at[k], d, p).wait_recv()
+        return carry
+
+    lax.fori_loop(0, 4, ratio_wait, 0)
+    summed = rbuf[0] + rbuf[1] + rbuf[2] + rbuf[3]
+    fit_out[...] = live_own / jnp.full((1, 512), cc_in[0], jnp.int32).astype(F32) * summed
+
+    def close_ratio(k, carry):
+        @pl.when(k != p)
+        def _():
+            ratio_copy(k).wait_send()
+
+        return carry
+
+    lax.fori_loop(0, 4, close_ratio, 0)
 
 
 def shards(points, cells, clone_weight, potential, support_count, cell_count):
@@ -621,6 +672,8 @@
             pltpu.VMEM((4, 8, 2048), F32),
             pltpu.VMEM((4, 8, 2048), F32),
             pltpu.VMEM((4, 8, 2048), F32),
+            pltpu.VMEM((16, 1024), BF16),
+            pltpu.VMEM((16, 1024), BF16),
             pltpu.VMEM((16, 1024), BF16),
             pltpu.VMEM((64, 512), F32),
             pltpu.VMEM((DEPTH, 2048), BF16),
@@ -647,6 +700,10 @@
             dma((4, 4)),
             dma((4,)),
             dma((4,)),
+            dma,
+            dma,
+            dma,
+            dma,
         ],
         compiler_params=pltpu.CompilerParams(
             collective_id=0, has_side_effects=True, vmem_limit_bytes=62 * 1024 * 1024

time: 102 us -> 100 us (0.980)
  Pallas kernels: 97.3 us -> 95 us
    pallas_call x1, Pallas kernels: 97.3 us -> 95 us  [shards(): pl.pallas_call(body, out_shape=(jax.ShapeDtypeStruct((2, 64, 512), F32),...]
where the time goes in v3:
time: 100 us; the launch traced here: 99.9 us
  Pallas kernels  95 us (95%)
  local copies, waits for them, and re-layouts  2.94 us (3%)
  between operations  1.93 us (2%)
    pallas_call x1, Pallas kernels, shards(): pl.pallas_call(body, out_shape=(jax.ShapeDtypeStruct((2, 64, 512), F32),...  95 us

profile of v3, /device:TPU:1, one launch (start us, length us, event | category | flops | bytes accessed | tf_op | source)
XLA Modules:
  0.0 99.9 jit_solution(17872895073753596975)
XLA Ops:
  1.9 95.0 %days.1 = (f32[2,64,512]{2,1,0:T(8,128)}, f32[1,512]{1,0:T(1,128)}) custom-call(bf16[1,64,512]{2,1,0:T(8,128)(2,1)} %pts_in.1, bf16[1,64,2048]{2,1,0:T(8,128)(2,1)} %cells_in.1, f32[1,64,512]{2,1,0:T(8,128)} %cw_in.1, f32[1,512]{1,0:T(1,128)} %pot_in.1, s32[1]{0:T(128)S(6)} %copy.10.sc_in, s32[1]{0:T(128)S(6)} %copy.11.cc_in), custom_call_target="tpu_custom_call" | custom-call | tf_op jit(solution)/shard_map/days/pallas_call | solution.py:659
  96.9 1.7 %fusion = (f32[1,64,512]{2,1,0:T(8,128)}, f32[1,64,512]{2,1,0:T(8,128)}) fusion(f32[2,64,512]{2,1,0:T(8,128)} %get-tuple-element.5), kind=kLoop, calls=%fused_computation | loop fusion | bytes 524288 | tf_op jit(solution)/shard_map/slice | solution.py:713
  98.6 0.0 copy-start
  98.6 0.7 copy-done
  99.3 0.6 copy.12
Async XLA Ops:
  98.6 0.7 copy-start

commit v4 on v3

--- a/solution.py
+++ b/solution.py
@@ -171,7 +171,8 @@
 
     def give():
         def turned(group):
-            return lax.rem(group + 2 * p + 2, GROUPS)
+            far = jnp.where(group < 4, 1 - bit, bit)
+            return 2 * lax.rem(p + 2 + lax.rem(group, 4), 4) + far
 
         lax.fori_loop(0, GROUPS, lambda n, carry: give_pts(turned(n), carry), 0)
         lax.fori_loop(0, GROUPS, lambda n, carry: give_wts(turned(n), carry), 0)
@@ -640,7 +641,7 @@
 
     lax.fori_loop(0, 4, ratio_wait, 0)
     summed = rbuf[0] + rbuf[1] + rbuf[2] + rbuf[3]
-    fit_out[...] = live_own / jnp.full((1, 512), cc_in[0], jnp.int32).astype(F32) * summed
+    fit_out[...] = summed
 
     def close_ratio(k, carry):
         @pl.when(k != p)
@@ -656,7 +657,7 @@
     vmem = pl.BlockSpec(memory_space=pltpu.VMEM)
     smem = pl.BlockSpec(memory_space=pltpu.SMEM)
     dma = pltpu.SemaphoreType.DMA
-    both, ratio = pl.pallas_call(
+    both, summed = pl.pallas_call(
         body,
         out_shape=(
             jax.ShapeDtypeStruct((2, 64, 512), F32),
@@ -710,7 +711,9 @@
         ),
         name="days",
     )(points, cells, clone_weight, potential, support_count, cell_count)
-    return both[0][None], both[1][None], ratio
+    slot = jnp.arange(512, dtype=jnp.int32)[None] + lax.axis_index("pt") * 512
+    live = (slot < support_count[0]).astype(F32)
+    return both[0][None], both[1][None], live / cell_count[0].astype(F32) * summed
 
 
 def solution(mesh):

time: 100 us -> 100 us (level)
  no operation moved by 1% of the time
where the time goes in v4:
time: 100 us; the launch traced here: 99.8 us
  Pallas kernels  94.9 us (95%)
  local copies, waits for them, and re-layouts  2.36 us (2%)
  between operations  1.99 us (2%)
    pallas_call x1, Pallas kernels, shards(): pl.pallas_call(body, out_shape=(jax.ShapeDtypeStruct((2, 64, 512), F32),...  94.9 us

profile of v4, /device:TPU:1, one launch (start us, length us, event | category | flops | bytes accessed | tf_op | source)
XLA Modules:
  0.0 99.8 jit_solution(9024424649866136309)
XLA Ops:
  1.9 94.9 %days.1 = (f32[2,64,512]{2,1,0:T(8,128)}, f32[1,512]{1,0:T(1,128)}) custom-call(bf16[1,64,512]{2,1,0:T(8,128)(2,1)} %pts_in.1, bf16[1,64,2048]{2,1,0:T(8,128)(2,1)} %cells_in.1, f32[1,64,512]{2,1,0:T(8,128)} %cw_in.1, f32[1,512]{1,0:T(1,128)} %pot_in.1, s32[1]{0:T(128)} %copy.9.sc_in, s32[1]{0:T(128)S(6)} %copy.10.cc_in), custom_call_target="tpu_custom_call" | custom-call | tf_op jit(solution)/shard_map/days/pallas_call | solution.py:660
  96.9 0.0 copy-start
  96.9 0.7 copy-done
  97.5 0.6 fusion
  98.1 1.7 %fusion.1 = (f32[1,64,512]{2,1,0:T(8,128)}, f32[1,64,512]{2,1,0:T(8,128)}) fusion(f32[2,64,512]{2,1,0:T(8,128)} %get-tuple-element.5), kind=kLoop, calls=%fused_computation.2 | loop fusion | bytes 524288 | tf_op jit(solution)/shard_map/slice | solution.py:716
Async XLA Ops:
  96.9 0.7 copy-start
